TPU v7x, 128 devices: a whole 4x4x4 slice. The times are simulated.
128 devices in a mesh: dp: 8 (over y, core), seq: 16 (over x, z).
Axes of the slice: x: 4, y: 4, z: 4, core: 2. Of those that a mesh axis runs over, the one named last changes fastest.
Arguments:
- query: bfloat16 [8, 2048, 1536], P('dp', 'seq'), may hold values from -6 to 6
- key_in: bfloat16 [8, 2048, 1536], P('dp', 'seq'), may hold values from -6 to 6
- value: bfloat16 [8, 2048, 1536], P('dp', 'seq'), may hold values from -6 to 6
- grad_out: bfloat16 [8, 2048, 1536], P('dp', 'seq'), may hold values from -6 to 6
- expert_ids: int32 [8, 2048, 2], P('dp', 'seq'), may hold values from 0 to 15, all different within a row; in each aligned block of 128 rows (0 to 127, 128 to 255, ..., all dimensions but the last counted through in order) at most 18 rows name the same one
- gate_weights: float32 [8, 2048, 2], P('dp', 'seq'), may hold values from 0.25 to 1
- w_gate: bfloat16 [16, 1536, 4096], P('seq', None, 'dp'), may hold values from -0.15625 to 0.15625
- w_up: bfloat16 [16, 1536, 4096], P('seq', None, 'dp'), may hold values from -0.15625 to 0.15625
- w_down: bfloat16 [16, 4096, 1536], P('seq', 'dp'), may hold values from -0.09375 to 0.09375
Outputs:
- grad_query: bfloat16 [8, 2048, 1536], P('dp', 'seq')
- grad_key: bfloat16 [8, 2048, 1536], P('dp', 'seq')
- grad_value: bfloat16 [8, 2048, 1536], P('dp', 'seq')
- grad_down: bfloat16 [16, 4096, 1536], P('seq', 'dp')
Inputs may be any that keep to these rules, and one draw needn't show every extreme that they name: `expert_ids`: each token names two different experts; among the 128 tokens of one device no expert is named more than 18 times, and in every draw some expert is named exactly 18 times by some device.
All inputs are finite; a program needn't handle non-finite values.
Results may differ from a plain program's by a relative error of at most 0.024.
Values may be sent and summed in bfloat16 or wider, within the bound.
A program may use at most 192 MiB of HBM per device.

v0:
```python
import jax
import jax.numpy as jnp
from jax import lax
from jax.experimental import pallas as pl
from jax.experimental.pallas import tpu as pltpu
from jax.sharding import PartitionSpec as P

bf = jnp.bfloat16
f32 = jnp.float32
MESH = pl.DeviceIdType.MESH
HD = 96
SC = HD ** -0.5
C2 = SC * 1.4426950408889634
VLIM = 62 << 20
ORDER = [1, 4, 3, 12, 5, 15, 7, 13, 8, 2, 9, 6, 11, 14, 10]


def nt(a, b):
    return lax.dot_general(a, b, (((1,), (1,)), ((), ())), preferred_element_type=f32)


def nn(a, b):
    return lax.dot_general(a, b, (((1,), (0,)), ((), ())), preferred_element_type=f32)


def tn(a, b):
    return lax.dot_general(a, b, (((0,), (0,)), ((), ())), preferred_element_type=f32)


def iota(shape, dim):
    return lax.broadcasted_iota(jnp.int32, shape, dim)


def onehot(cond):
    return jnp.where(cond, 1.0, 0.0).astype(bf)


class Place:
    def __init__(self):
        self.dp = lax.axis_index("dp")
        self.s = lax.axis_index("seq")
        self.x = self.s // 4
        self.z = lax.rem(self.s, 4)
        self.y = self.dp // 2
        self.core = lax.rem(self.dp, 2)

    def to(self, o):
        dx, dz = o // 4, lax.rem(o, 4) if not isinstance(o, int) else o % 4
        return lax.rem(self.x + dx, 4) * 4 + lax.rem(self.z + dz, 4)

    def source(self, o):
        dx, dz = o // 4, lax.rem(o, 4) if not isinstance(o, int) else o % 4
        return lax.rem(self.x + 4 - dx, 4) * 4 + lax.rem(self.z + 4 - dz, 4)

    def clip(self, k):
        return lax.rem(self.y + k, 4) * 2 + self.core

    def pair(self, k):
        return lax.rem(self.y + k, 4) * 2 + 1 - self.core


def greet(devices):
    b = pltpu.get_barrier_semaphore()
    for d in devices:
        pl.semaphore_signal(b, inc=1, device_id=d, device_id_type=MESH)


def greeted(n):
    pl.semaphore_wait(pltpu.get_barrier_semaphore(), n)


def rcopy(src, dst, ss, rs, dev):
    return pltpu.make_async_remote_copy(
        src_ref=src, dst_ref=dst, send_sem=ss, recv_sem=rs, device_id=dev, device_id_type=MESH
    )


class Exchange:
    def __init__(self, at, send, recv, ss, rs):
        self.at, self.send, self.recv, self.ss, self.rs = at, send, recv, ss, rs

    def out(self, o):
        t = self.at.to(o)
        return rcopy(self.send(t), self.recv(self.at.s), self.ss.at[o], self.rs.at[o], (self.at.dp, t))

    def into(self, o):
        t = self.at.source(o)
        return rcopy(self.send(t), self.recv(t), self.ss.at[o], self.rs.at[o], (self.at.dp, t))

    def start(self):
        for o in ORDER:
            self.out(o).start()

    def wait_recv(self):
        @pl.loop(1, 16)
        def _(o):
            self.into(o).wait_recv()

    def wait_send(self):
        @pl.loop(1, 16)
        def _(o):
            self.out(o).wait_send()


def seq_peers(at):
    return [(at.dp, at.to(o)) for o in ORDER]


def dp_peers(at):
    return [(at.clip(1), at.s), (at.clip(3), at.s), (at.clip(2), at.s), (at.pair(0), at.s)]


def main_places(M, b):
    io = iota((256, 128), 0).astype(f32)
    return onehot((io == M[b, 0:1, :]) | (io == M[b, 1:2, :]))


def extra_places(M, b):
    io = iota((512, 128), 0)
    low = lax.rem(io, 32)
    own = (low // 2) == b
    tgt = ((io // 32) * 2 + lax.rem(io, 2)).astype(f32)
    return onehot(own & ((tgt == M[b, 2:3, :]) | (tgt == M[b, 3:4, :])))


class Gather:
    def __init__(self, at, buf, base, pieces, ss, rs):
        self.at, self.buf, self.base, self.pieces, self.ss, self.rs = at, buf, base, pieces, ss, rs

    def copy(self, n, c, i, dev):
        rows, cols = self.pieces[i]
        ref = self.buf.at[self.base + c, rows, cols]
        return rcopy(ref, ref, self.ss.at[n], self.rs.at[n], (dev, self.at.s))

    def own_out(self, i):
        a = self.at
        self.copy(i, a.clip(0), i, a.clip(1)).start()
        self.copy(2 + i, a.clip(0), i, a.clip(3)).start()
        self.copy(6 + i, a.clip(0), i, a.pair(0)).start()

    def near(self, i):
        a = self.at
        self.copy(i, a.clip(3), i, a.clip(1)).wait_recv()
        if i == 0:
            self.copy(4, a.clip(3), 0, a.clip(1)).start()
        self.copy(8 + i, a.clip(3), i, a.pair(0)).start()
        self.copy(2 + i, a.clip(1), i, a.clip(3)).wait_recv()
        if i == 1:
            self.copy(5, a.clip(1), 1, a.clip(3)).start()
        self.copy(10 + i, a.clip(1), i, a.pair(0)).start()

    def far(self):
        a = self.at
        for i in (0, 1):
            self.copy(4 + i, a.clip(2), i, a.clip(1)).wait_recv()
            self.copy(12 + i, a.clip(2), i, a.pair(0)).start()

    def other(self, k):
        n = {0: 6, 3: 8, 1: 10, 2: 12}[k]
        for i in (0, 1):
            self.copy(n + i, self.at.pair(k), i, self.at.pair(0)).wait_recv()

    def wait_send(self):
        for n in range(14):
            i = {4: 0, 5: 1}.get(n, n % 2)
            self.copy(n, self.at.clip(0), i, self.at.clip(1)).wait_send()


def scores(j, Q, K, ET, s_ref):
    CH = 512
    q0 = pl.multiple_of(j * 256, 256)
    Qj = Q[pl.ds(q0, 256), :]
    m = None
    for c in range(2048 // CH):
        s = nt(K[c * CH:(c + 1) * CH, :], Qj)
        s_ref[c * CH:(c + 1) * CH, :] = s
        mc = jnp.max(s.reshape(CH // 8, 8, 256), axis=0)
        m = mc if m is None else jnp.maximum(m, mc)
    m = jnp.max(m, axis=0, keepdims=True) * C2
    for c in range(2048 // CH):
        e = jnp.exp2(s_ref[c * CH:(c + 1) * CH, :] * C2 - m).astype(bf)
        ET[c * CH:(c + 1) * CH, pl.ds(q0, 256)] = e


def mix(j, Vt, ET, Oa, mixed):
    q0 = pl.multiple_of(j * 256, 256)
    ot = nn(Vt[...], ET[:, pl.ds(q0, 256)])
    linv = 1.0 / ot[96:97, :]
    on = jnp.concatenate([ot[:96, :] * linv, jnp.broadcast_to(linv, (32, 256))], axis=0)
    o = on.T
    Oa[pl.ds(q0, 256), :] = o
    mixed[pl.ds(q0, 256), :] = o.astype(bf)


def dscores(j, dO, V, Kt, ET, Oa, AG, dOs):
    r = pl.ds(pl.multiple_of(256 * j, 256), 256)
    d = dO[r, :96].astype(f32)
    oa = Oa[r, :]
    dOs[r, :] = jnp.concatenate([(d * oa[:, 96:97]).astype(bf), jnp.zeros((256, 32), bf)], axis=1)
    delta = -jnp.sum(d * oa[:, :96], axis=1, keepdims=True)
    hi = delta.astype(bf)
    rest = delta - hi.astype(f32)
    mid = rest.astype(bf)
    lo = (rest - mid.astype(f32)).astype(bf)
    daug = jnp.concatenate([d.astype(bf), hi, mid, lo, jnp.zeros((256, 29), bf)], axis=1)
    dqt = None
    for kb in range(8):
        ks = slice(256 * kb, 256 * kb + 256)
        ds = ET[ks, r] * nt(V[ks, :], daug).astype(bf)
        slot = jnp.where(j < 6, kb, 8 + kb // 3)
        lane = jnp.where(j < 6, 256 * j, 512 * (kb % 3) + 256 * (j - 6))
        AG[slot, 0:256, pl.ds(pl.multiple_of(lane, 256), 256)] = ds
        term = nn(Kt[:, ks], ds)
        dqt = term if dqt is None else dqt + term
    return (dqt.T * (oa[:, 96:97] * SC)).astype(bf)


def block(q, k, v, go, ids, gws, wg_hbm, wu_hbm, wd_hbm, R, grad_down,
          S, SG, RG, Ms, M, SM, RM, SX, RX, B, RB, RB2, wg, wu, wd, AG, ET, Q, K, V, T, X, Qs, Oa, s_ref,
          ACT, DG, PT, SR, SS, RR, gd,
          ss_x, rs_x, ss_y, rs_y, ss_m, rs_m, ss_s, rs_s, ss_e, rs_e, ss_b, rs_b, ss_c, rs_c, ss_g, rs_g, ss_h, rs_h,
          ss_p, rs_p, ss_r, rs_r, sem_w):
    at = Place()
    greet(seq_peers(at) + dp_peers(at))
    weights = [pltpu.make_async_copy(a, b, sem_w.at[n])
               for n, (a, b) in enumerate(((wg_hbm, wg), (wu_hbm, wu), (wd_hbm, wd)))]

    e0, e1 = ids[0:1, :].astype(f32), ids[1:2, :].astype(f32)
    g0, g1 = gws[0:1, :], gws[1:2, :]
    ie = iota((16, 128), 0).astype(f32)
    oh0, oh1 = jnp.where(ie == e0, 1.0, 0.0), jnp.where(ie == e1, 1.0, 0.0)
    before = onehot(iota((128, 128), 0) < iota((128, 128), 1))
    count = nn((oh0 + oh1).astype(bf), before)
    s0 = jnp.sum(oh0 * count, axis=0, keepdims=True)
    s1 = jnp.sum(oh1 * count, axis=0, keepdims=True)
    m0 = jnp.where(s0 < 16, e0 * 16 + s0, -1.0)
    m1 = jnp.where(s1 < 16, e1 * 16 + s1, -1.0)
    x0 = jnp.where(s0 < 16, -1.0, e0 * 2 + s0 - 16)
    x1 = jnp.where(s1 < 16, -1.0, e1 * 2 + s1 - 16)
    Ms[...] = jnp.concatenate([m0, m1, x0, x1, m0, m0, m0, m0], axis=0)

    io = iota((256, 128), 0).astype(f32)
    c0, c1 = io == m0, io == m1
    gw = jnp.sum(jnp.where(c0, g0, 0.0) + jnp.where(c1, g1, 0.0), axis=1, keepdims=True)
    pm = onehot(c0 | c1)
    for n in range(3):
        cols = slice(512 * n, 512 * n + 512)
        SM[:, :, cols] = (nn(pm, go[:, cols]) * gw).astype(bf).reshape(16, 16, 512)
    io = iota((32, 128), 0).astype(f32)
    c0, c1 = io == x0, io == x1
    gw = jnp.sum(jnp.where(c0, g0, 0.0) + jnp.where(c1, g1, 0.0), axis=1, keepdims=True)
    ext = (nn(onehot(c0 | c1), go[...]) * gw).astype(bf)
    stack = jnp.concatenate([ext[:, 128 * g:128 * g + 128] for g in range(12)], axis=0)
    r, c = iota((512, 384), 0), iota((512, 384), 1)
    low = lax.rem(r, 32)
    spread = onehot(c == (low // 2) * 32 + (r // 32) * 2 + lax.rem(low, 2))
    SX[...] = nn(spread, stack).astype(bf).reshape(16, 32, 128)

    xm = Exchange(at, lambda t: Ms, lambda t: M.at[t], ss_m, rs_m)
    halves = [pl.ds(0, 768), pl.ds(768, 768)]
    xs = [Exchange(at, lambda t, c=c: SM.at[t, :, c], lambda t, c=c: RM.at[t, :, c], ss_s.at[n], rs_s.at[n])
          for n, c in enumerate(halves)]
    xe = Exchange(at, lambda t: SX.at[t], lambda t: RX.at[t], ss_e, rs_e)
    xq = [Exchange(at, lambda t, n=n: S.at[n, t], lambda t, n=n: R.at[n, t], ss_x.at[n], rs_x.at[n])
          for n in range(3)]
    xg = Exchange(at, lambda t: SG.at[t], lambda t: RG.at[t], ss_x.at[3], rs_x.at[3])

    def pack(ref, put):
        for h in range(16):
            put(h, jnp.concatenate(
                [ref[32 * g:32 * g + 32, 96 * h:96 * h + 96] for g in range(4)], axis=1))

    greeted(19)
    xe.start()
    for e in xs:
        e.start()
    for n, ref in ((1, k), (0, q), (2, v)):
        def put(h, w):
            S[n, h] = w
        pack(ref, put)
        R[n, at.s] = S[n, at.s]
        if n < 2:
            xq[n].start()
    xm.start()

    def put_g(h, w):
        SG[h] = w
    pack(go, put_g)
    RG[at.s] = SG[at.s]
    for w in weights:
        w.start()
    M[at.s] = Ms[...]
    RM[at.s] = SM[at.s]
    RX[at.s] = SX[at.s]

    r, c = iota((384, 512), 1), iota((384, 512), 0)
    low = lax.rem(r, 32)
    pick = onehot(c == (low // 2) * 32 + (r // 32) * 2 + lax.rem(low, 2))
    xe.wait_recv()
    back = nn(pick, RX[...].reshape(512, 128)).astype(bf)
    AG[at.dp, 256:288, :] = jnp.concatenate([back[32 * g:32 * g + 32] for g in range(12)], axis=1)
    gs = Gather(at, AG, 0, [(pl.ds(0, 288), c) for c in halves], ss_g, rs_g)
    for i in (0, 1):
        xs[i].wait_recv()
        cols = slice(768 * i, 768 * i + 768)
        AG[at.dp, 0:256, cols] = RM[:, :, cols].reshape(256, 768)
        gs.own_out(i)

    def unpack(n, dst, fill):
        @pl.loop(0, 16)
        def _(b):
            w = R[n, b]
            for g in range(4):
                dst[pl.ds(pl.multiple_of(b * 128 + 32 * g, 32), 32), :] = jnp.concatenate(
                    [w[:, 96 * g:96 * g + 96], jnp.full((32, 32), fill, bf)], axis=1)

    xq[1].wait_recv()
    unpack(1, K, 0)
    xq[0].wait_recv()
    xq[2].start()
    unpack(0, Q, 0)

    @pl.loop(0, 8)
    def _(j):
        scores(j, Q, K, ET, s_ref)
    gs.near(0)
    xq[2].wait_recv()
    unpack(2, V, 1)
    T[...] = V[...].T
    xm.wait_recv()

    xb = []
    for part in range(3):
        cols = pl.ds(384 * part, 384 if part < 2 else 128)
        xb.append(Exchange(at, lambda t, cols=cols: B.at[t, :, cols], lambda t, cols=cols: RB.at[t, :, cols],
                           ss_b.at[part], rs_b.at[part]))
    for part in (0, 1):
        @pl.loop(4 * part, 4 * part + 4)
        def _(j):
            mix(j, T, ET, Oa, X)
        for j in range(4 * part, 4 * part + 4):
            for i in (0, 1):
                b = 2 * j + i
                w = nn(main_places(M, b), X[128 * b:128 * b + 128, :]).astype(bf)
                B[:, 16 * i:16 * i + 16, 96 * j:96 * j + 96] = w[:, :96].reshape(16, 16, 96)
        xb[part].start()
    acc = jnp.zeros((512, 128), f32)
    for b in range(16):
        acc = acc + nn(extra_places(M, b), X[128 * b:128 * b + 128, :])
    B[:, :, 768:864] = acc[:, :96].astype(bf).reshape(16, 32, 96)
    B[:, :, 864:896] = jnp.zeros((16, 32, 32), bf)
    xb[2].start()
    RB[at.s] = B[at.s]
    xg.start()
    gs.near(1)
    T[...] = K[...].T
    Qs[...] = (Q[...].astype(f32) * (Oa[:, 96:97] * SC)).astype(bf)

    mine = 8 + at.dp
    gr = Gather(at, AG, 8, [(pl.ds(0, 128), pl.ds(0, 1536)), (pl.ds(128, 160), pl.ds(0, 1536))], ss_h, rs_h)
    for part in range(3):
        xb[part].wait_recv()
        for j in range(4 * part, min(4 * part + 4, 9)):
            AG[mine, 32 * j:32 * j + 32, :] = jnp.concatenate(
                [RB[h, :, 96 * j:96 * j + 96] for h in range(16)], axis=1)
        if part == 0:
            gr.own_out(0)
    gr.own_out(1)
    gs.far()
    for kk in range(4):
        gs.other(kk)
    for w in weights:
        w.wait()

    def chunk(c, slot):
        for f in range(2):
            fs = slice(256 * f, 256 * f + 256)
            rows = AG[8 + c]
            gate = nn(rows, wg[:, fs])
            up = nn(rows, wu[:, fs])
            dact = nt(AG[c], wd[fs, :])
            sig = 1.0 / (1.0 + jnp.exp(-gate))
            silu = gate * sig
            ACT[c, :, fs] = (silu * up).astype(bf)
            DG[:, 256 * f:256 * f + 256] = (dact * up * (sig * (1.0 + gate * (1.0 - sig)))).astype(bf)
            DG[:, 512 + 256 * f:768 + 256 * f] = (dact * silu).astype(bf)
        for n in range(3):
            ns = slice(512 * n, 512 * n + 512)
            PT[slot, :, ns] = (nt(DG[:, :512], wg[ns, :]) + nt(DG[:, 512:], wu[ns, :])).astype(bf)

    def sib(k, slot):
        return rcopy(PT.at[slot], SR.at[k], ss_p.at[k], rs_p.at[k], (at.pair(0), at.s))

    order = (0, 1, 3, 2)

    def work(k):
        n = order.index(k)
        if n >= 2:
            sib(order[n - 2], n % 2).wait_send()
        chunk(at.pair(k), n % 2)
        sib(k, n % 2).start()
        chunk(at.clip(k), 2)
        sib(k, n % 2).wait_recv()
        SS[k] = (PT[2].astype(f32) + SR[k].astype(f32)).astype(bf)

    FIRST, SECOND = ((0, 64), (64, 80)), ((192, 96), (144, 48))
    msg = {}

    def add_messages(name, k, parts, to):
        for i, (lo, size) in enumerate(parts):
            msg[name + "ab"[i]] = (k, pl.ds(lo, size), to, len(msg), pl.ds(lo % 144, size))

    add_messages("d1", 1, SECOND, 1)
    add_messages("d3", 3, FIRST, 3)
    add_messages("r1", 2, FIRST, 1)
    add_messages("r3", 2, SECOND, 3)
    add_messages("f1", 1, FIRST, 1)
    add_messages("f3", 3, SECOND, 3)

    def hop(name):
        k, rows, to, n, land = msg[name]
        return rcopy(SS.at[k, rows, :], RR.at[n // 2, land, :], ss_r.at[n], rs_r.at[n], (at.clip(to), at.s))

    def start(name):
        for i in "ab":
            hop(name + i).start()

    def plus(k, rows, *names):
        term = SS[k, rows, :].astype(f32)
        for name in names:
            term = term + RR[msg[name][3] // 2, msg[name][4], :].astype(f32)
        SS[k, rows, :] = term.astype(bf)

    gr.other(0)
    work(0)
    gr.near(0)
    gr.near(1)
    gr.other(1)
    work(1)
    start("d1")
    gr.other(3)
    work(3)
    start("d3")
    gr.far()
    gr.other(2)
    work(2)
    start("r1")
    start("r3")
    acts = ACT[...].reshape(2304, 512)
    for n in range(3):
        ns = slice(512 * n, 512 * n + 512)
        gd[:, ns] = tn(acts, AG[0:8, :, ns].reshape(2304, 512)).astype(bf)
    gd_copy = pltpu.make_async_copy(gd, grad_down, sem_w.at[0])
    gd_copy.start()
    for i in "ab":
        for r, f in (("r1", "f1"), ("r3", "f3")):
            hop(r + i).wait_recv()
            plus(msg[f + i][0], msg[f + i][1], r + i)
            hop(f + i).start()
    for e in xb + xq:
        e.wait_send()
    gs.wait_send()
    gr.wait_send()

    GROUPS = {0: (0, 1, 6, 7), 2: (8,), 1: (2, 3, 4, 5)}
    xc = {}
    for part in (0, 2, 1):
        lanes = 384 if part < 2 else 128
        cols = pl.ds(384 * part, lanes)
        xc[part] = Exchange(at, lambda t, cols=cols: B.at[t, :, cols], lambda t, cols=cols: RB2.at[t, :, cols],
                            ss_c.at[part], rs_c.at[part])
        if part < 2:
            for direct, relayed in (("d3", "f1"), ("d1", "f3")):
                names = [direct + "ab"[part], relayed + "ab"[part]]
                for name in names:
                    hop(name).wait_recv()
                plus(0, msg[names[0]][1], *names)
        for h in range(16):
            parts = [SS[0, 32 * j:32 * j + 32, 96 * h:96 * h + 96] for j in GROUPS[part]]
            if part == 2:
                parts.append(jnp.zeros((32, 32), bf))
            B[h, :, 384 * part:384 * part + lanes] = jnp.concatenate(parts, axis=1)
        xc[part].start()
    RB2[at.s] = B[at.s]
    xg.wait_recv()

    def dmixed(part):
        extra = RB2[:, :, 768:896].reshape(512, 128)
        for n, j in enumerate(GROUPS[part]):
            for i in (0, 1):
                b = 2 * j + i
                lane = 384 * part + 96 * n
                t = slice(128 * b, 128 * b + 128)
                w = RB2[:, 16 * i:16 * i + 16, lane:lane + 96].reshape(256, 96)
                gb = jnp.concatenate([RG[b, :, 96 * g:96 * g + 96] for g in range(4)], axis=0).astype(f32)
                dm = gb + (tn(main_places(M, b), w) + tn(extra_places(M, b), extra)[:, :96])
                X[t, :] = jnp.concatenate([dm.astype(bf), jnp.zeros((128, 32), bf)], axis=1)

    dOs = Q
    def message(n, source, target):
        return rcopy(S.at[n, target], R.at[n, source], ss_y.at[n, target], rs_y.at[n, source], (at.dp, target))

    def lay(n, rows, b):
        S[n, b] = jnp.concatenate([rows[32 * g:32 * g + 32, :96] for g in range(4)], axis=1)

    def post(n, rows, first, count):
        for i in range(count):
            b = first + i
            lay(n, rows[128 * i:128 * i + 128, :], b)

            @pl.when(b != at.s)
            def _():
                message(n, at.s, b).start()

            @pl.when(b == at.s)
            def _():
                R[n, b] = S[n, b]

    def queries(first, step):
        @pl.loop(0, 4)
        def _(i):
            j = first + i + step * (i // 2)
            dq = dscores(j, X, V, T, ET, Oa, AG, dOs)
            for n in (0, 1):
                lay(0, dq[128 * n:128 * n + 128, :], 2 * j + n)

    for part in (0, 2):
        xc[part].wait_recv()
    dmixed(0)
    queries(0, 4)
    xc[1].wait_recv()
    dmixed(1)
    queries(2, 0)
    R[0, at.s] = S[0, at.s]
    for o in ORDER:
        message(0, at.s, at.to(o)).start()

    @pl.loop(0, 4)
    def _(i):
        j = lax.rem(i + at.s // 4, 4)
        rows = pl.ds(pl.multiple_of(j * 512, 512), 512)
        post(2, nn(ET[rows, :], dOs[...]).astype(bf), 4 * j, 4)

    @pl.loop(0, 8)
    def _(i):
        kb = lax.rem(i + at.s // 2, 8)
        lane = pl.ds(pl.multiple_of(512 * lax.rem(kb, 3), 512), 512)
        dk = nn(AG[kb, 0:256, :], Qs[0:1536, :]) + nn(AG[8 + kb // 3, 0:256, lane], Qs[1536:2048, :])
        post(1, dk.astype(bf), 2 * kb, 2)

    @pl.loop(1, 16)
    def _(o):
        t = at.source(o)
        for n in range(3):
            message(n, t, t).wait_recv()

    @pl.loop(1, 16)
    def _(o):
        t = at.to(o)
        for n in range(3):
            message(n, at.s, t).wait_send()

    for e in [xm, xe, xg] + xs + [xc[part] for part in range(3)]:
        e.wait_send()
    for k, n in ((3, 0), (2, 1)):
        sib(k, n).wait_send()
    for name in msg:
        hop(name).wait_send()
    gd_copy.wait()


def results(R, gd, gq, gk, gv, gd_out):
    for n, dst in enumerate((gq, gk, gv)):
        for g in range(4):
            dst[32 * g:32 * g + 32, :] = jnp.concatenate(
                [R[n, h, :, 96 * g:96 * g + 96] for h in range(16)], axis=1)
    gd_out[...] = gd[...]


def vm(*shape, dtype=bf):
    return pltpu.VMEM(shape, dtype)


def dma(*shape):
    return pltpu.SemaphoreType.DMA(shape)


def sds(*shape):
    return jax.ShapeDtypeStruct(shape, bf)


ANY = pl.BlockSpec(memory_space=pl.ANY)
VM = pl.BlockSpec(memory_space=pltpu.VMEM)


def per_device(query, key_in, value, grad_out, expert_ids, gate_weights, w_gate, w_up, w_down):
    head = [vm(2048, 128)] * 3 + [vm(128, 2048)] + [vm(2048, 128)] * 2
    R, gd = pl.pallas_call(
        block,
        out_shape=[sds(3, 16, 32, 384), sds(512, 1536)],
        in_specs=[VM] * 6 + [ANY] * 3,
        out_specs=[VM, ANY],
        scratch_shapes=[
            vm(3, 16, 32, 384), vm(16, 32, 384), vm(16, 32, 384), vm(8, 128, dtype=f32), vm(16, 8, 128, dtype=f32),
            vm(16, 16, 1536), vm(16, 16, 1536), vm(16, 32, 128), vm(16, 32, 128),
            vm(16, 32, 896), vm(16, 32, 896), vm(16, 32, 896),
            vm(1536, 512), vm(1536, 512), vm(512, 1536), vm(16, 288, 1536), vm(2048, 2048)]
        + head + [vm(2048, 128, dtype=f32), vm(2048, 256, dtype=f32),
                  vm(8, 288, 512), vm(288, 1024), vm(3, 288, 1536), vm(4, 288, 1536), vm(4, 288, 1536),
                  vm(6, 144, 1536), vm(512, 1536)]
        + [dma(4, 16)] * 2 + [dma(3, 16)] * 2 + [dma(16)] * 2 + [dma(2, 16)] * 2 + [dma(16)] * 2 + [dma(3, 16)] * 4 + [dma(14)] * 4
        + [dma(4)] * 2 + [dma(12)] * 2 + [dma(3)],
        name="block",
        compiler_params=pltpu.CompilerParams(collective_id=0, has_side_effects=True, vmem_limit_bytes=VLIM),
    )(query[0], key_in[0], value[0], grad_out[0], expert_ids[0].T, gate_weights[0].T, w_gate[0], w_up[0], w_down[0])
    gq, gk, gv, gd = pl.pallas_call(
        results,
        out_shape=[sds(128, 1536)] * 3 + [sds(512, 1536)],
        name="results",
    )(R, gd)
    return (gq[None], gk[None], gv[None], gd[None])


def solution(mesh):
    seq = P("dp", "seq", None)
    return jax.shard_map(
        per_device,
        mesh=mesh,
        in_specs=(seq,) * 6 + (P("seq", None, "dp"), P("seq", None, "dp"), P("seq", "dp", None)),
        out_specs=(seq, seq, seq, P("seq", "dp", None)),
        check_vma=False,
    )
```

profile of v0, /device:TPU:10, one launch (start us, length us, event | category | flops | bytes accessed | tf_op | source)
XLA Modules:
  0.0 165.0 jit_solution(2842045950040402838)
XLA Ops:
  0.6 160.8 %block.1 = (bf16[3,16,32,384]{3,2,1,0:T(8,128)(2,1)}, bf16[512,1536]{1,0:T(8,128)(2,1)}) custom-call(bf16[128,1536]{1,0:T(8,128)(2,1)} %bitcast.20, bf16[128,1536]{1,0:T(8,128)(2,1)} %bitcast.21, bf16[128,1536]{1,0:T(8,128)(2,1)} %bitcast.22, bf16[128,1536]{1,0:T(8,128)(2,1)} %bitcast.23, s32[2,128]{1,0:T(2,128)} %bitcast.24, f32[2,128]{1,0:T(2,128)} %bitcast.25, ...), custom_call_target="tpu_custom_call" | custom-call | tf_op jit(solution)/shard_map/block/pallas_call | solution.py:598
  161.4 3.6 %results.1 = (bf16[128,1536]{1,0:T(8,128)(2,1)}, bf16[128,1536]{1,0:T(8,128)(2,1)}, bf16[128,1536]{1,0:T(8,128)(2,1)}, bf16[512,1536]{1,0:T(8,128)(2,1)}) custom-call(bf16[3,16,32,384]{3,2,1,0:T(8,128)(2,1)} %get-tuple-element.10.R, bf16[512,1536]{1,0:T(8,128)(2,1)} %get-tuple-element.11.gd), custom_call_target="tpu_custom_call" | custom-call | tf_op jit(solution)/shard_map/results/pallas_call | solution.py:616
where the time goes:
time: 166 us; the launch traced here: 165 us
  Pallas kernels  164 us (99%)
    pallas_call x1, Pallas kernels, per_device(): pl.pallas_call(block, out_shape=[sds(3, 16, 32, 384), sds(512, 1536)], in...  161 us
    pallas_call x1, Pallas kernels, per_device(): pl.pallas_call(results, out_shape=[sds(128, 1536)] * 3 + [sds(512, 1536)]...  3.59 us

commit v1 on v0

--- a/solution.py
+++ b/solution.py
@@ -192,7 +192,7 @@
     mixed[pl.ds(q0, 256), :] = o.astype(bf)
 
 
-def dscores(j, dO, V, Kt, ET, Oa, AG, dOs):
+def dscores(j, dO, V, ET, Oa, AG, dOs):
     r = pl.ds(pl.multiple_of(256 * j, 256), 256)
     d = dO[r, :96].astype(f32)
     oa = Oa[r, :]
@@ -203,16 +203,23 @@
     mid = rest.astype(bf)
     lo = (rest - mid.astype(f32)).astype(bf)
     daug = jnp.concatenate([d.astype(bf), hi, mid, lo, jnp.zeros((256, 29), bf)], axis=1)
-    dqt = None
     for kb in range(8):
         ks = slice(256 * kb, 256 * kb + 256)
         ds = ET[ks, r] * nt(V[ks, :], daug).astype(bf)
         slot = jnp.where(j < 6, kb, 8 + kb // 3)
         lane = jnp.where(j < 6, 256 * j, 512 * (kb % 3) + 256 * (j - 6))
         AG[slot, 0:256, pl.ds(pl.multiple_of(lane, 256), 256)] = ds
-        term = nn(Kt[:, ks], ds)
+
+
+def dqueries(j, Kt, Oa, AG):
+    r = pl.ds(pl.multiple_of(256 * j, 256), 256)
+    dqt = None
+    for kb in range(8):
+        slot = jnp.where(j < 6, kb, 8 + kb // 3)
+        lane = jnp.where(j < 6, 256 * j, 512 * (kb % 3) + 256 * (j - 6))
+        term = nn(Kt[:, 256 * kb:256 * kb + 256], AG[slot, 0:256, pl.ds(pl.multiple_of(lane, 256), 256)])
         dqt = term if dqt is None else dqt + term
-    return (dqt.T * (oa[:, 96:97] * SC)).astype(bf)
+    return (dqt.T * (Oa[r, 96:97] * SC)).astype(bf)
 
 
 def block(q, k, v, go, ids, gws, wg_hbm, wu_hbm, wd_hbm, R, grad_down,
@@ -344,6 +351,8 @@
                 w = nn(main_places(M, b), X[128 * b:128 * b + 128, :]).astype(bf)
                 B[:, 16 * i:16 * i + 16, 96 * j:96 * j + 96] = w[:, :96].reshape(16, 16, 96)
         xb[part].start()
+        if part == 0:
+            gs.near(1)
     acc = jnp.zeros((512, 128), f32)
     for b in range(16):
         acc = acc + nn(extra_places(M, b), X[128 * b:128 * b + 128, :])
@@ -352,7 +361,6 @@
     xb[2].start()
     RB[at.s] = B[at.s]
     xg.start()
-    gs.near(1)
     T[...] = K[...].T
     Qs[...] = (Q[...].astype(f32) * (Oa[:, 96:97] * SC)).astype(bf)
 
@@ -503,37 +511,52 @@
     def lay(n, rows, b):
         S[n, b] = jnp.concatenate([rows[32 * g:32 * g + 32, :96] for g in range(4)], axis=1)
 
+    def go_out(n, b):
+        @pl.when(b != at.s)
+        def _():
+            message(n, at.s, b).start()
+
+        @pl.when(b == at.s)
+        def _():
+            R[n, b] = S[n, b]
+
     def post(n, rows, first, count):
         for i in range(count):
-            b = first + i
-            lay(n, rows[128 * i:128 * i + 128, :], b)
-
-            @pl.when(b != at.s)
-            def _():
-                message(n, at.s, b).start()
-
-            @pl.when(b == at.s)
-            def _():
-                R[n, b] = S[n, b]
-
-    def queries(first, step):
-        @pl.loop(0, 4)
-        def _(i):
-            j = first + i + step * (i // 2)
-            dq = dscores(j, X, V, T, ET, Oa, AG, dOs)
-            for n in (0, 1):
-                lay(0, dq[128 * n:128 * n + 128, :], 2 * j + n)
+            lay(n, rows[128 * i:128 * i + 128, :], first + i)
+            go_out(n, first + i)
 
     for part in (0, 2):
         xc[part].wait_recv()
     dmixed(0)
-    queries(0, 4)
+
+    @pl.loop(0, 4)
+    def _(i):
+        dscores(i + 4 * (i // 2), X, V, ET, Oa, AG, dOs)
+
+    @pl.loop(0, 4)
+    def _(i):
+        j = i + 4 * (i // 2)
+        dq = dqueries(j, T, Oa, AG)
+        for n in (0, 1):
+            lay(0, dq[128 * n:128 * n + 128, :], 2 * j + n)
+
     xc[1].wait_recv()
+
+    @pl.loop(0, 8)
+    def _(i):
+        n = lax.rem(i + at.s, 8)
+        go_out(0, n + 8 * (n // 4))
+
     dmixed(1)
-    queries(2, 0)
-    R[0, at.s] = S[0, at.s]
-    for o in ORDER:
-        message(0, at.s, at.to(o)).start()
+
+    @pl.loop(0, 4)
+    def _(i):
+        dscores(2 + i, X, V, ET, Oa, AG, dOs)
+
+    @pl.loop(0, 4)
+    def _(i):
+        j = 2 + lax.rem(i + at.s, 4)
+        post(0, dqueries(j, T, Oa, AG), 2 * j, 2)
 
     @pl.loop(0, 4)
     def _(i):

time: 166 us -> 160 us (0.964)
  Pallas kernels: 164 us -> 159 us
    pallas_call x1, Pallas kernels: 161 us -> 156 us  [per_device(): pl.pallas_call(block, out_shape=[sds(3, 16, 32, 384), sds(512, 1536)], in...]
where the time goes in v1:
time: 160 us
  Pallas kernels  159 us (99%)
    pallas_call x1, Pallas kernels, per_device(): pl.pallas_call(block, out_shape=[sds(3, 16, 32, 384), sds(512, 1536)], in...  156 us
    pallas_call x1, Pallas kernels, per_device(): pl.pallas_call(results, out_shape=[sds(128, 1536)] * 3 + [sds(512, 1536)]...  3.59 us

profile of v1, /device:TPU:10, one launch (start us, length us, event | category | flops | bytes accessed | tf_op | source)
XLA Modules:
  0.0 160.0 jit_solution(17041006276160706974)
XLA Ops:
  0.6 155.7 %block.1 = (bf16[3,16,32,384]{3,2,1,0:T(8,128)(2,1)}, bf16[512,1536]{1,0:T(8,128)(2,1)}) custom-call(bf16[128,1536]{1,0:T(8,128)(2,1)} %bitcast.20, bf16[128,1536]{1,0:T(8,128)(2,1)} %bitcast.21, bf16[128,1536]{1,0:T(8,128)(2,1)} %bitcast.22, bf16[128,1536]{1,0:T(8,128)(2,1)} %bitcast.23, s32[2,128]{1,0:T(2,128)} %bitcast.24, f32[2,128]{1,0:T(2,128)} %bitcast.25, ...), custom_call_target="tpu_custom_call" | custom-call | tf_op jit(solution)/shard_map/block/pallas_call | solution.py:621
  156.4 3.6 %results.1 = (bf16[128,1536]{1,0:T(8,128)(2,1)}, bf16[128,1536]{1,0:T(8,128)(2,1)}, bf16[128,1536]{1,0:T(8,128)(2,1)}, bf16[512,1536]{1,0:T(8,128)(2,1)}) custom-call(bf16[3,16,32,384]{3,2,1,0:T(8,128)(2,1)} %get-tuple-element.10.R, bf16[512,1536]{1,0:T(8,128)(2,1)} %get-tuple-element.11.gd), custom_call_target="tpu_custom_call" | custom-call | tf_op jit(solution)/shard_map/results/pallas_call | solution.py:639
